TPU v7x, 256 devices: a whole 4x4x8 slice. The times are simulated.
256 devices in a mesh: dp: 16 (over x, y), tensor: 16 (over z, core).
Axes of the slice: x: 4, y: 4, z: 8, core: 2. Of those that a mesh axis runs over, the one named last changes fastest.
Arguments:
- acts: bfloat16 [32, 512, 16384], P('dp', None, 'tensor'), may hold values from -6 to 6
- grads: bfloat16 [32, 512, 53248], P('dp', None, 'tensor'), may hold values from -6 to 6
- proj_in: bfloat16 [16384, 64], P('tensor'), may hold values from -0.046875 to 0.046875
- proj_out: bfloat16 [53248, 64], P('tensor'), may hold values from -0.02734375 to 0.02734375
- lengths: int32 [32], P('dp'), may hold values from 64 to 512, as said below
- queries: int32 [16], replicated, may hold values from 0 to 31, as said below
Outputs:
- blocks: float32 [32, 4096], P('dp', 'tensor')
- scores: float32 [32, 16], P('dp')
Inputs may be any that keep to these rules, and one draw needn't show every extreme that they name: `lengths`: some example has exactly 512 tokens in use and some exactly 64. `queries`: all distinct; 0 and 31 are among them.
All inputs are finite; a program needn't handle non-finite values.
Results may differ from a plain program's by a relative error of at most 0.0003.
Values sent between devices are 32-bit elements; how exact they have to be, the bound alone decides.
No kernel may reach another device: no remote copies, remote signals or barrier semaphores. Data moves between devices by JAX's collectives and lax.ppermute only.
A program may use at most 64 MiB of HBM per device.

v0:
```python
import jax
import jax.numpy as jnp
from jax import lax
from jax.sharding import PartitionSpec as P


def body(acts, grads, proj_in, proj_out, lengths, queries):
    highest = lax.Precision.HIGHEST
    examples, seq, width_in = acts.shape
    width_out = grads.shape[2]
    rank = proj_in.shape[1]
    total_rows = examples * seq
    scale = seq ** (-0.5)
    act_rows = acts.reshape(total_rows, width_in)
    grad_rows = grads.reshape(total_rows, width_out)
    shards = lax.axis_size("tensor")
    columns = rank * rank // shards
    out_part = jnp.dot(grad_rows, proj_out, preferred_element_type=jnp.float32)
    in_part = jnp.dot(act_rows, proj_in, preferred_element_type=jnp.float32)
    summed = lax.psum(jnp.concatenate([out_part, in_part], axis=1), "tensor")
    keep = (jnp.arange(seq, dtype=jnp.int32)[None, :] < lengths[:, None]).astype(jnp.float32)
    out_rows = summed[:, :rank].reshape(examples, seq, rank) * keep[:, :, None]
    in_rows = summed[:, rank:].reshape(examples, seq, rank)
    full_blocks = jnp.einsum("esi,esj->eij", out_rows, in_rows, precision=highest) * scale
    full_blocks = full_blocks.reshape(examples, rank * rank)
    own_blocks = lax.dynamic_slice_in_dim(
        full_blocks, lax.axis_index("tensor") * columns, columns, 1
    )
    piece = lax.all_gather(full_blocks, "dp", axis=0, tiled=True)
    ids = jnp.arange(piece.shape[0], dtype=jnp.int32)
    select = (queries[:, None] == ids[None, :]).astype(jnp.float32)
    chosen = jnp.dot(select, piece, precision=highest)
    scores = jnp.dot(full_blocks, chosen.T, precision=highest) / rank
    return (own_blocks, scores)


def solution(mesh):
    return jax.shard_map(
        body,
        mesh=mesh,
        in_specs=(
            P("dp", None, "tensor"),
            P("dp", None, "tensor"),
            P("tensor", None),
            P("tensor", None),
            P("dp"),
            P(),
        ),
        out_specs=(P("dp", "tensor"), P("dp", None)),
        check_vma=False,
    )
```

profile of v0, /device:TPU:2, one launch (start us, length us, event | category | flops | bytes accessed | tf_op | source)
XLA Modules:
  0.0 163.6 jit_solution(362226926997445474)
XLA Ops:
  7.2 0.0 copy-start
  7.2 0.0 copy-start.1
  7.2 0.0 all-reduce.2.cloned.1.call-start
  7.2 1.5 copy-done
  8.8 1.7 %fusion.8 = f32[1024,64]{0,1:T(8,128)S(1)} fusion(bf16[1024,1024]{1,0:T(8,128)(2,1)S(1)} %bitcast.17, bf16[1024,64]{0,1:T(8,128)(2,1)} %param.8), kind=kOutput, calls=%fused_computation.15 | convolution fusion | flops 134217728 | bytes 2490368 | tf_op jit(solution)/shard_map/dot_general | solution.py:19
  10.4 0.0 copy-start.2
  10.4 5.2 %fusion.7 = f32[1024,64]{0,1:T(8,128)S(1)} fusion(bf16[1024,3328]{1,0:T(8,128)(2,1)} %bitcast.18, bf16[3328,64]{0,1:T(8,128)(2,1)} %param.9), kind=kOutput, calls=%fused_computation.14 | convolution fusion | flops 436207616 | bytes 7503872 | tf_op jit(solution)/shard_map/dot_general | solution.py:18
  15.6 0.8 pad_maximum_fusion
  16.4 0.0 all-reduce.2.cloned.1.call-update
  16.5 0.0 copy-done.1
  16.5 0.1 compare_convert_fusion
  16.5 112.7 %all-reduce.2.cloned.1.call-done = f32[1024,128]{0,1:T(8,128)} async-done(((f32[1024,128]{0,1:T(8,128)}), f32[1024,128]{0,1:T(8,128)}) %all-reduce.2.cloned.1.call-update) | async-done | bytes 524304 | tf_op jit(solution)/shard_map/psum | solution.py:20
  129.2 1.1 fusion.6
  130.3 0.4 convolution_multiply_fusion
  130.7 0.1 reshape.46
  130.8 0.1 reshape.47
  130.9 23.7 %all-gather = f32[16,2,4096]{2,1,0:T(2,128)S(1)} all-gather(f32[1,2,4096]{2,1,0:T(2,128)S(1)} %reshape.47), channel_id=1, replica_groups=mesh['dp'=16,'tensor'=16] {'dp'}, dimensions={0}, use_global_device_ids=true | all-gather | bytes 557056 | tf_op jit(solution)/shard_map/all_gather | solution.py:29
  154.5 0.4 reshape.48
  154.9 0.6 constant_dynamic-slice_fusion
  155.5 0.0 copy-done.2
  155.5 0.3 fusion.4
  155.8 1.0 convolution_multiply_fusion.1
Async XLA Ops:
  7.2 1.6 copy-start
  7.2 9.3 %copy-start.1 = (s32[2]{0:T(128)S(1)}, s32[2]{0:T(128)}, u32[]{:S(2)}) copy-start(s32[2]{0:T(128)} %param.10) | copy-start | bytes 28
  7.2 122.0 %all-reduce.2.cloned.1.call-start = ((), (), s32[]{:S(2)}) async-start(), calls=%async_computation | async-start | bytes 1048576 | tf_op jit(solution)/shard_map/psum | solution.py:20
  10.4 145.0 %copy-start.2 = (s32[16]{0:T(128)S(1)}, s32[16]{0:T(128)}, u32[]{:S(2)}) copy-start(s32[16]{0:T(128)} %param.11) | copy-start | bytes 196
Sparse Core Ops, SparseCore 0:
  16.6 112.5 all-reduce.1
where the time goes:
time: 164 us
  waiting for transfers between devices  113 us (69%)
  blocking collectives  23.7 us (14%)
  between operations  14.1 us (9%)
  matrix products  8.5 us (5%)
  local copies, waits for them, and re-layouts  3.74 us (2%)
    psum x1, waiting for transfers between devices, body(): summed = lax.psum(jnp.concatenate([out_part, in_part], axis=1), 'tensor')  113 us
    all_gather x1, blocking collectives, body(): piece = lax.all_gather(full_blocks, 'dp', axis=0, tiled=True)  23.7 us
    dot_general x1, matrix products, body(): out_part = jnp.dot(grad_rows, proj_out, preferred_element_type=jnp.float32)  5.16 us
  transfers between devices with their start and end apart: 1, of which 1 were waited for; matrix products, arithmetic and copies ran while one was open for 0% of the time, Pallas kernels for 0%

commit v1 on v0

v1 whole, which is shorter than its diff:
```python
import functools

import jax
import jax.numpy as jnp
from jax import lax
from jax.experimental import pallas as pl
from jax.experimental.pallas import tpu as pltpu
from jax.sharding import Mesh, PartitionSpec as P

F32 = jnp.float32
HIGHEST = lax.Precision.HIGHEST
VMEM_BYTES = 16 * 1024 * 1024
ALL_VMEM = 60 * 1024 * 1024
NT = (((1,), (1,)), ((), ()))
TN = (((0,), (0,)), ((), ()))


def vmem():
    return pl.BlockSpec(memory_space=pltpu.VMEM)


def smem():
    return pl.BlockSpec(memory_space=pltpu.SMEM)


def params(limit=VMEM_BYTES):
    return pltpu.CompilerParams(vmem_limit_bytes=limit)


def project_kernel(which, grads, acts, w_out, w_in, out):
    del which
    left = lax.dot_general(grads[0], w_out[...], NT, preferred_element_type=F32)
    right = lax.dot_general(acts[0], w_in[...], NT, preferred_element_type=F32)
    out[...] = jnp.concatenate([left, right], axis=1)


def project(which, grads, acts, w_out, w_in, tile=128):
    _, seq, width_out = grads.shape
    width_in = acts.shape[2]
    rank = w_out.shape[0]
    return pl.pallas_call(
        project_kernel,
        grid_spec=pltpu.PrefetchScalarGridSpec(
            num_scalar_prefetch=1,
            grid=(seq // tile,),
            in_specs=[
                pl.BlockSpec((1, tile, width_out), lambda r, which: (which[0], r, 0)),
                pl.BlockSpec((1, tile, width_in), lambda r, which: (which[0], r, 0)),
                pl.BlockSpec((rank, width_out), lambda r, which: (0, 0)),
                pl.BlockSpec((rank, width_in), lambda r, which: (0, 0)),
            ],
            out_specs=pl.BlockSpec((tile, 2 * rank), lambda r, which: (r, 0)),
        ),
        out_shape=jax.ShapeDtypeStruct((seq, 2 * rank), F32),
        compiler_params=params(ALL_VMEM),
        cost_estimate=pl.CostEstimate(
            flops=2 * seq * rank * (width_in + width_out),
            bytes_accessed=2 * (seq + rank) * (width_in + width_out) + 8 * seq * rank,
            transcendentals=0,
        ),
        name="project",
    )(which, grads, acts, w_out, w_in)


def outer_kernel(scale, count, pieces, out, square):
    rows = jnp.sum(pieces[...], axis=0)
    tokens, width = rows.shape
    rank = width // 2
    keep = (lax.broadcasted_iota(jnp.int32, (tokens, rank), 0) < count[0]).astype(F32)
    square[...] = scale * lax.dot_general(
        rows[:, :rank] * keep, rows[:, rank:], TN, precision=HIGHEST, preferred_element_type=F32
    )
    even = square[pl.ds(0, rank // 2, stride=2), :]
    odd = square[pl.ds(1, rank // 2, stride=2), :]
    flat = jnp.concatenate([even, odd], axis=1)
    out[...] = jnp.broadcast_to(flat[None], out.shape)


def outer(count, pieces, scale):
    shards, _, width = pieces.shape
    rank = width // 2
    return pl.pallas_call(
        functools.partial(outer_kernel, scale),
        in_specs=[smem(), vmem()],
        out_specs=vmem(),
        out_shape=jax.ShapeDtypeStruct((shards, rank // 2, width), F32),
        scratch_shapes=[pltpu.VMEM((rank, rank), F32)],
        compiler_params=params(),
        name="outer",
    )(count, pieces)


def total_kernel(pieces, own, copies):
    block = jnp.sum(pieces[...], axis=0)
    own[...] = block
    copies[...] = jnp.broadcast_to(block[None], copies.shape)


def total(pieces, groups):
    _, rows, width = pieces.shape
    return pl.pallas_call(
        total_kernel,
        in_specs=[vmem()],
        out_specs=[vmem(), vmem()],
        out_shape=[
            jax.ShapeDtypeStruct((rows, width), F32),
            jax.ShapeDtypeStruct((groups, rows, width), F32),
        ],
        compiler_params=params(),
        name="total",
    )(pieces)


def score_kernel(place, queries, own, other, gathered, own_blocks, scores):
    core = place[0]
    start = 2 * place[1]
    rank = 2 * own.shape[0]
    mine, theirs = own[...], other[...]
    pair = (jnp.where(core == 0, mine, theirs), jnp.where(core == 0, theirs, mine))
    for e in range(2):
        ref = (own, other)
        first = [r[pl.ds(start, 1), :] for r in ref]
        second = [r[pl.ds(start + 1, 1), :] for r in ref]
        pick = core == e
        own_blocks[pl.ds(e, 1), :] = jnp.concatenate(
            [jnp.where(pick, first[0], first[1]), jnp.where(pick, second[0], second[1])], axis=1
        )
    blocks = gathered[...]
    groups = blocks.shape[0]
    ids = 2 * lax.broadcasted_iota(jnp.int32, (groups, queries.shape[1]), 0) + core
    select = (ids == queries[...]).astype(F32)
    for e in range(2):
        products = jnp.sum(blocks * pair[e][None], axis=1)
        dots = jnp.sum(products, axis=1, keepdims=True)
        scores[pl.ds(e, 1), :] = jnp.sum(dots * select, axis=0, keepdims=True) / rank


def score(place, queries, own, other, gathered):
    width = own.shape[1]
    return pl.pallas_call(
        score_kernel,
        in_specs=[smem(), vmem(), vmem(), vmem(), vmem()],
        out_specs=[vmem(), vmem()],
        out_shape=[
            jax.ShapeDtypeStruct((2, 2 * width), F32),
            jax.ShapeDtypeStruct((2, queries.shape[0]), F32),
        ],
        compiler_params=params(),
        name="score",
    )(place, queries.reshape(1, -1), own, other, gathered)


SWAP = [(0, 1), (1, 0)]


def body(acts, grads, proj_in, proj_out, lengths, queries):
    seq = acts.shape[1]
    core = lax.axis_index("core").astype(jnp.int32)
    z = lax.axis_index("z").astype(jnp.int32)
    depth = lax.axis_size("z")
    groups = lax.axis_size("x") * lax.axis_size("y")
    w_out, w_in = proj_out.T, proj_in.T
    theirs = project((1 - core)[None], grads, acts, w_out, w_in)
    received = lax.ppermute(theirs, "core", SWAP)
    mine = project(core[None], grads, acts, w_out, w_in)
    rows = (mine + received).reshape(depth, seq // depth, mine.shape[1])
    pieces = lax.all_to_all(rows, "z", 0, 0)
    count = (jnp.where(core == 0, lengths[0], lengths[1]) - z * (seq // depth))[None]
    spread = outer(count, pieces, seq ** (-0.5))
    parts = lax.all_to_all(spread, "z", 0, 0)
    own, copies = total(parts, groups)
    other = lax.ppermute(own, "core", SWAP)
    gathered = lax.all_to_all(copies, ("x", "y"), 0, 0)
    place = jnp.stack([core, 2 * z + core])
    own_blocks, part = score(place, queries, own, other, gathered)
    scores = part + lax.ppermute(part, "core", SWAP)
    return own_blocks, scores


def solution(mesh):
    devices = mesh.devices.reshape(4, 4, 8, 2)
    dp, tensor = ("x", "y"), ("z", "core")
    return jax.shard_map(
        body,
        mesh=Mesh(devices, dp + tensor),
        in_specs=(
            P(dp, None, tensor),
            P(dp, None, tensor),
            P(tensor, None),
            P(tensor, None),
            P(dp),
            P(),
        ),
        out_specs=(P(dp, tensor), P(dp, None)),
        check_vma=False,
    )
```

time: 164 us -> 66.4 us (0.40)
  the two profiles are of different devices: /device:TPU:2 before, /device:TPU:1 now
where the time goes in v1:
time: 66.4 us; the launch traced here: 65.9 us
  starting transfers between devices  21.9 us (33%)
  waiting for transfers between devices  16.4 us (25%)
  Pallas kernels  12.1 us (18%)
  blocking collectives  10.6 us (16%)
  other arithmetic  2.34 us (4%)
  between operations  2 us (3%)
    all_to_all x1, blocking collectives, body(): parts = lax.all_to_all(spread, 'z', 0, 0)  10.6 us
    all_to_all x1, waiting for transfers between devices, body(): pieces = lax.all_to_all(rows, 'z', 0, 0)  10.4 us
    pallas_call x2, Pallas kernels, project(): pl.pallas_call(project_kernel, grid_spec=pltpu.PrefetchScalarGridSpec(num...  9.81 us
    all_to_all x1, starting transfers between devices, body(): gathered = lax.all_to_all(copies, ('x', 'y'), 0, 0)  6.75 us
    all_to_all x1, starting transfers between devices, body(): pieces = lax.all_to_all(rows, 'z', 0, 0)  6.45 us
    all_to_all x1, waiting for transfers between devices, body(): gathered = lax.all_to_all(copies, ('x', 'y'), 0, 0)  4.33 us
    ppermute x1, starting transfers between devices, body(): received = lax.ppermute(theirs, 'core', SWAP)  3.32 us
    ppermute x1, starting transfers between devices, body(): scores = part + lax.ppermute(part, 'core', SWAP)  3.2 us
  transfers between devices with their start and end apart: 5, of which 4 were waited for; matrix products, arithmetic and copies ran while one was open for 1% of the time, Pallas kernels for 7%

profile of v1, /device:TPU:1, one launch (start us, length us, event | category | flops | bytes accessed | tf_op | source)
XLA Modules:
  0.0 65.9 jit_solution(17438763575290089302)
XLA Ops:
  0.6 4.9 %project.3 = f32[512,128]{1,0:T(8,128)} custom-call(s32[1]{0:T(128)} %bitcast.8.which, bf16[2,512,3328]{2,1,0:T(8,128)(2,1)} %grads.3, bf16[2,512,1024]{2,1,0:T(8,128)(2,1)} %acts.3, bf16[64,3328]{1,0:T(8,128)(2,1)} %bitcast.11, bf16[64,1024]{1,0:T(8,128)(2,1)} %bitcast.13), custom_call_target="tpu_custom_call" | custom-call | flops 285212672 | bytes 5275648 | tf_op jit(solution)/shard_map/project/pallas_call | solution.py:41
  5.5 0.0 copy-start.1
  5.6 0.0 copy-start
  5.6 3.3 %collective-permute-start = (f32[512,128]{1,0:T(8,128)}, f32[512,128]{1,0:T(8,128)S(1)}, u32[]{:S(2)}, u32[]{:S(2)}) collective-permute-start(f32[512,128]{1,0:T(8,128)} %project.3), channel_id=1, source_target_pairs={{0,1},{1,0},{2,3},{3,2},{4,5},{5,4},{6,7},{7,6},{8,9},{9,8},{10,11... | collective-permute-start | bytes 786440 | tf_op jit(solution)/shard_map/ppermute | solution.py:164
  8.9 4.9 %project.2 = f32[512,128]{1,0:T(8,128)} custom-call(s32[1]{0:T(128)} %bitcast.which, bf16[2,512,3328]{2,1,0:T(8,128)(2,1)} %grads.3, bf16[2,512,1024]{2,1,0:T(8,128)(2,1)} %acts.3, bf16[64,3328]{1,0:T(8,128)(2,1)} %bitcast.12, bf16[64,1024]{1,0:T(8,128)(2,1)} %bitcast.14), custom_call_target="tpu_custom_call" | custom-call | flops 285212672 | bytes 5275648 | tf_op jit(solution)/shard_map/project/pallas_call | solution.py:41
  13.8 0.0 collective-permute-done
  13.8 1.7 %add.10 = f32[512,128]{1,0:T(8,128)} add(f32[512,128]{1,0:T(8,128)} %project.2, f32[512,128]{1,0:T(8,128)S(1)} %collective-permute-done) | non-fusion elementwise | flops 65536 | bytes 786432 | tf_op jit(solution)/shard_map/add | solution.py:166
  15.5 6.4 %all-to-all-start = ((f32[8,64,128]{2,1,0:T(8,128)}), f32[8,64,128]{2,1,0:T(8,128)S(1)}, u32[]{:S(2)}, u32[]{:S(2)}) async-start(f32[8,64,128]{2,1,0:T(8,128)} %bitcast.9), calls=%async_computation | async-start | bytes 524288 | tf_op jit(solution)/shard_map/all_to_all | solution.py:167
  21.9 0.0 copy-done.1
  21.9 0.6 fusion
  23.8 10.4 %all-to-all-done.pieces = f32[8,64,128]{2,1,0:T(8,128)S(1)} async-done(((f32[8,64,128]{2,1,0:T(8,128)}), f32[8,64,128]{2,1,0:T(8,128)S(1)}, u32[]{:S(2)}, u32[]{:S(2)}) %all-to-all-start) | async-done | bytes 262176 | tf_op jit(solution)/shard_map/all_to_all | solution.py:167
  34.3 0.3 outer.1
  34.6 10.6 %all_to_all.15.pieces = f32[8,32,128]{2,1,0:T(8,128)S(1)} all-to-all(f32[8,32,128]{2,1,0:T(8,128)S(1)} %outer.1), channel_id=1, replica_groups=mesh['x'=4,'y'=4,'z'=8,'core'=2] {'z'}, dimensions={0} | all-to-all | bytes 262144 | tf_op jit(solution)/shard_map/all_to_all | solution.py:170
  45.2 0.7 %total.1 = (f32[32,128]{1,0:T(8,128)S(1)}, f32[16,32,128]{2,1,0:T(8,128)}) custom-call(f32[8,32,128]{2,1,0:T(8,128)S(1)} %all_to_all.15.pieces), custom_call_target="tpu_custom_call" | custom-call | tf_op jit(solution)/shard_map/total/pallas_call | solution.py:101
  45.9 6.8 %all-to-all-start.2 = ((f32[16,32,128]{2,1,0:T(8,128)}), f32[16,32,128]{2,1,0:T(8,128)S(1)}, u32[]{:S(2)}, u32[]{:S(2)}) async-start(f32[16,32,128]{2,1,0:T(8,128)} %get-tuple-element.7), calls=%async_computation.2 | async-start | bytes 524288 | tf_op jit(solution)/shard_map/all_to_all | solution.py:173
  52.7 2.2 %collective-permute-start.1 = (f32[32,128]{1,0:T(8,128)S(1)}, f32[32,128]{1,0:T(8,128)S(1)}, u32[]{:S(2)}, u32[]{:S(2)}) collective-permute-start(f32[32,128]{1,0:T(8,128)S(1)} %get-tuple-element.6.own), channel_id=1, source_target_pairs={{0,1},{1,0},{2,3},{3,2},{4,5},{5,4},{6,7},{7,6},{8,9},{9,8},{10,11... | collective-permute-start | bytes 49160 | tf_op jit(solution)/shard_map/ppermute | solution.py:172
  54.9 0.1 pad_add_fusion.place
  55.0 0.8 %collective-permute-done.1.other = f32[32,128]{1,0:T(8,128)S(1)} collective-permute-done((f32[32,128]{1,0:T(8,128)S(1)}, f32[32,128]{1,0:T(8,128)S(1)}, u32[]{:S(2)}, u32[]{:S(2)}) %collective-permute-start.1) | collective-permute-done | bytes 16416 | tf_op jit(solution)/shard_map/ppermute | solution.py:172
  55.7 4.3 %all-to-all-done.2.gathered = f32[16,32,128]{2,1,0:T(8,128)S(1)} async-done(((f32[16,32,128]{2,1,0:T(8,128)}), f32[16,32,128]{2,1,0:T(8,128)S(1)}, u32[]{:S(2)}, u32[]{:S(2)}) %all-to-all-start.2) | async-done | bytes 262176 | tf_op jit(solution)/shard_map/all_to_all | solution.py:173
  60.1 0.0 copy-done
  60.1 1.2 %score.1 = (f32[2,256]{1,0:T(2,128)}, f32[2,16]{1,0:T(2,128)S(1)}) custom-call(s32[2]{0:T(128)S(1)} %pad_add_fusion.place, s32[1,16]{1,0:T(1,128)S(1)} %bitcast.10, f32[32,128]{1,0:T(8,128)S(1)} %get-tuple-element.6.own, f32[32,128]{1,0:T(8,128)S(1)} %collective-permute-done.1.other, f32[16,32,128]{2,1,0:T(8,128)S(1)} %all-to-all-done.2.gathered), custom_call_target="tpu_custom_call" | custom-call | tf_op jit(solution)/shard_map/score/pallas_call | solution.py:140
  61.3 3.2 %collective-permute-start.2 = (f32[2,16]{1,0:T(2,128)S(1)}, f32[2,16]{1,0:T(2,128)S(1)}, u32[]{:S(2)}, u32[]{:S(2)}) collective-permute-start(f32[2,16]{1,0:T(2,128)S(1)} %get-tuple-element.9), channel_id=1, source_target_pairs={{0,1},{1,0},{2,3},{3,2},{4,5},{5,4},{6,7},{7,6},{8,9},{9,8},{10,11... | collective-permute-start | bytes 392 | tf_op jit(solution)/shard_map/ppermute | solution.py:176
  64.5 0.8 %collective-permute-done.2 = f32[2,16]{1,0:T(2,128)S(1)} collective-permute-done((f32[2,16]{1,0:T(2,128)S(1)}, f32[2,16]{1,0:T(2,128)S(1)}, u32[]{:S(2)}, u32[]{:S(2)}) %collective-permute-start.2) | collective-permute-done | bytes 160 | tf_op jit(solution)/shard_map/ppermute | solution.py:176
  65.3 0.6 add.11
Async XLA Ops:
  5.5 16.4 %copy-start.1 = (s32[2]{0:T(128)S(1)}, s32[2]{0:T(128)}, u32[]{:S(2)}) copy-start(s32[2]{0:T(128)} %param.10) | copy-start | bytes 28
  5.6 54.5 %copy-start = (s32[16]{0:T(128)S(1)}, s32[16]{0:T(128)}, u32[]{:S(2)}) copy-start(s32[16]{0:T(128)} %param.11) | copy-start | bytes 196
  5.6 8.2 %collective-permute-start = (f32[512,128]{1,0:T(8,128)}, f32[512,128]{1,0:T(8,128)S(1)}, u32[]{:S(2)}, u32[]{:S(2)}) collective-permute-start(f32[512,128]{1,0:T(8,128)} %project.3), channel_id=1, source_target_pairs={{0,1},{1,0},{2,3},{3,2},{4,5},{5,4},{6,7},{7,6},{8,9},{9,8},{10,11... | collective-permute-start | bytes 786440 | tf_op jit(solution)/shard_map/ppermute | solution.py:164
  15.5 18.8 %all-to-all-start = ((f32[8,64,128]{2,1,0:T(8,128)}), f32[8,64,128]{2,1,0:T(8,128)S(1)}, u32[]{:S(2)}, u32[]{:S(2)}) async-start(f32[8,64,128]{2,1,0:T(8,128)} %bitcast.9), calls=%async_computation | async-start | bytes 524288 | tf_op jit(solution)/shard_map/all_to_all | solution.py:167
  45.9 14.1 %all-to-all-start.2 = ((f32[16,32,128]{2,1,0:T(8,128)}), f32[16,32,128]{2,1,0:T(8,128)S(1)}, u32[]{:S(2)}, u32[]{:S(2)}) async-start(f32[16,32,128]{2,1,0:T(8,128)} %get-tuple-element.7), calls=%async_computation.2 | async-start | bytes 524288 | tf_op jit(solution)/shard_map/all_to_all | solution.py:173
  52.7 3.0 %collective-permute-start.1 = (f32[32,128]{1,0:T(8,128)S(1)}, f32[32,128]{1,0:T(8,128)S(1)}, u32[]{:S(2)}, u32[]{:S(2)}) collective-permute-start(f32[32,128]{1,0:T(8,128)S(1)} %get-tuple-element.6.own), channel_id=1, source_target_pairs={{0,1},{1,0},{2,3},{3,2},{4,5},{5,4},{6,7},{7,6},{8,9},{9,8},{10,11... | collective-permute-start | bytes 49160 | tf_op jit(solution)/shard_map/ppermute | solution.py:172
  61.3 4.0 %collective-permute-start.2 = (f32[2,16]{1,0:T(2,128)S(1)}, f32[2,16]{1,0:T(2,128)S(1)}, u32[]{:S(2)}, u32[]{:S(2)}) collective-permute-start(f32[2,16]{1,0:T(2,128)S(1)} %get-tuple-element.9), channel_id=1, source_target_pairs={{0,1},{1,0},{2,3},{3,2},{4,5},{5,4},{6,7},{7,6},{8,9},{9,8},{10,11... | collective-permute-start | bytes 392 | tf_op jit(solution)/shard_map/ppermute | solution.py:176

commit v2 on v1

v2 whole, which is shorter than its diff:
```python
import functools

import jax
import jax.numpy as jnp
from jax import lax
from jax.experimental import pallas as pl
from jax.experimental.pallas import tpu as pltpu
from jax.sharding import Mesh, PartitionSpec as P

F32 = jnp.float32
HIGHEST = lax.Precision.HIGHEST
VMEM_BYTES = 24 * 1024 * 1024
NT = (((1,), (1,)), ((), ()))
TN = (((0,), (0,)), ((), ()))


def vmem():
    return pl.BlockSpec(memory_space=pltpu.VMEM)


def params():
    return pltpu.CompilerParams(vmem_limit_bytes=VMEM_BYTES)


def in_hbm(x):
    return pltpu.with_memory_space_constraint(x, pltpu.HBM)


def project_kernel(grads, acts, w_out, w_in, out):
    rank = w_out.shape[0]
    out[:, rank:] = lax.dot_general(acts[0], w_in[...], NT, preferred_element_type=F32)
    out[:, :rank] = lax.dot_general(grads[0], w_out[...], NT, preferred_element_type=F32)


def project(which, grads, acts, w_out, w_in, tile=256):
    _, seq, width_out = grads.shape
    width_in = acts.shape[2]
    rank = w_out.shape[0]
    return pl.pallas_call(
        project_kernel,
        grid=(seq // tile,),
        in_specs=[
            pl.BlockSpec((1, tile, width_out), lambda r: (which(), r, 0)),
            pl.BlockSpec((1, tile, width_in), lambda r: (which(), r, 0)),
            pl.BlockSpec((rank, width_out), lambda r: (0, 0)),
            pl.BlockSpec((rank, width_in), lambda r: (0, 0)),
        ],
        out_specs=pl.BlockSpec((tile, 2 * rank), lambda r: (r, 0)),
        out_shape=jax.ShapeDtypeStruct((seq, 2 * rank), F32),
        compiler_params=params(),
        cost_estimate=pl.CostEstimate(
            flops=2 * seq * rank * (width_in + width_out),
            bytes_accessed=2 * (seq + rank) * (width_in + width_out) + 8 * seq * rank,
            transcendentals=0,
        ),
        name="project",
    )(in_hbm(grads), in_hbm(acts), in_hbm(w_out), in_hbm(w_in))


def outer_kernel(scale, lengths, pieces, out, square):
    rows = jnp.sum(pieces[...], axis=0)
    tokens, width = rows.shape
    rank = width // 2
    core, z = lax.axis_index("core"), lax.axis_index("z")
    count = jnp.where(core == 0, lengths[:, :1], lengths[:, 1:2])
    token = lax.broadcasted_iota(jnp.int32, (tokens, rank), 0) + z * tokens
    keep = (token < count).astype(F32)
    square[...] = scale * lax.dot_general(
        rows[:, :rank] * keep, rows[:, rank:], TN, precision=HIGHEST, preferred_element_type=F32
    )
    even = square[pl.ds(0, rank // 2, stride=2), :]
    odd = square[pl.ds(1, rank // 2, stride=2), :]
    flat = jnp.concatenate([even, odd], axis=1)
    out[...] = jnp.broadcast_to(flat[None], out.shape)


def outer(lengths, pieces, scale):
    shards, _, width = pieces.shape
    rank = width // 2
    return pl.pallas_call(
        functools.partial(outer_kernel, scale),
        in_specs=[vmem(), vmem()],
        out_specs=vmem(),
        out_shape=jax.ShapeDtypeStruct((shards, rank // 2, width), F32),
        scratch_shapes=[pltpu.VMEM((rank, rank), F32)],
        compiler_params=params(),
        name="outer",
    )(lengths.reshape(1, -1), pieces)


def total_kernel(pieces, own):
    own[...] = jnp.sum(pieces[...], axis=0)


def total(pieces):
    return pl.pallas_call(
        total_kernel,
        in_specs=[vmem()],
        out_specs=vmem(),
        out_shape=jax.ShapeDtypeStruct(pieces.shape[1:], F32),
        compiler_params=params(),
        name="total",
    )(pieces)


def keep_kernel(own, other, out):
    core = lax.axis_index("core")
    start = 2 * (2 * lax.axis_index("z") + core)
    first = [r[pl.ds(start, 1), :] for r in (own, other)]
    second = [r[pl.ds(start + 1, 1), :] for r in (own, other)]
    for e in range(2):
        pick = core == e
        out[pl.ds(e, 1), :] = jnp.concatenate(
            [jnp.where(pick, first[0], first[1]), jnp.where(pick, second[0], second[1])], axis=1
        )


def keep_columns(own, other):
    return pl.pallas_call(
        keep_kernel,
        in_specs=[vmem(), vmem()],
        out_specs=vmem(),
        out_shape=jax.ShapeDtypeStruct((2, 2 * own.shape[1]), F32),
        compiler_params=params(),
        name="keep_columns",
    )(own, other)


def score_kernel(queries, own, other, gathered, scores):
    core = lax.axis_index("core")
    rank = 2 * own.shape[0]
    mine, theirs = own[...], other[...]
    pair = (jnp.where(core == 0, mine, theirs), jnp.where(core == 0, theirs, mine))
    blocks = gathered[...]
    groups = blocks.shape[0]
    ids = 2 * lax.broadcasted_iota(jnp.int32, (groups, queries.shape[1]), 0) + core
    select = (ids == queries[...]).astype(F32)
    for e in range(2):
        products = jnp.sum(blocks * pair[e][None], axis=1)
        dots = jnp.sum(products, axis=1, keepdims=True)
        scores[pl.ds(e, 1), :] = jnp.sum(dots * select, axis=0, keepdims=True) / rank


def score(queries, own, other, gathered):
    return pl.pallas_call(
        score_kernel,
        in_specs=[vmem(), vmem(), vmem(), vmem()],
        out_specs=vmem(),
        out_shape=jax.ShapeDtypeStruct((2, queries.shape[0]), F32),
        compiler_params=params(),
        name="score",
    )(queries.reshape(1, -1), own, other, gathered)


SWAP = [(0, 1), (1, 0)]


def body(acts, grads, proj_in, proj_out, lengths, queries):
    seq = acts.shape[1]
    depth = lax.axis_size("z")
    groups = lax.axis_size("x") * lax.axis_size("y")
    w_out, w_in = proj_out.T, proj_in.T
    theirs = project(lambda: 1 - lax.axis_index("core"), grads, acts, w_out, w_in)
    received = lax.ppermute(theirs, "core", SWAP)
    mine = project(lambda: lax.axis_index("core"), grads, acts, w_out, w_in)
    rows = (mine + received).reshape(depth, seq // depth, mine.shape[1])
    pieces = lax.all_to_all(rows, "z", 0, 0)
    spread = outer(lengths, pieces, seq ** (-0.5))
    parts = lax.all_to_all(spread, "z", 0, 0)
    own = total(parts)
    other = lax.ppermute(own, "core", SWAP)
    copies = jnp.broadcast_to(own[None], (groups,) + own.shape)
    gathered = lax.all_to_all(copies, ("x", "y"), 0, 0)
    own_blocks = keep_columns(own, other)
    part = score(queries, own, other, gathered)
    scores = part + lax.ppermute(part, "core", SWAP)
    return own_blocks, scores


def solution(mesh):
    devices = mesh.devices.reshape(4, 4, 8, 2)
    dp, tensor = ("x", "y"), ("z", "core")
    return jax.shard_map(
        body,
        mesh=Mesh(devices, dp + tensor),
        in_specs=(
            P(dp, None, tensor),
            P(dp, None, tensor),
            P(tensor, None),
            P(tensor, None),
            P(dp),
            P(),
        ),
        out_specs=(P(dp, tensor), P(dp, None)),
        check_vma=False,
    )
```

time: 66.4 us -> 60.2 us (0.907)
  blocking collectives: 10.6 us -> 29.2 us
  waiting for transfers between devices: 16.4 us -> 5.41 us
  starting transfers between devices: 21.9 us -> 15.6 us
  Pallas kernels: 12.1 us -> 7.68 us
  other arithmetic: 2.34 us -> 0.6 us
  between operations: 2 us -> 0.69 us
    all_to_all x0 -> x1, blocking collectives: none -> 18.6 us  [body(): pieces = lax.all_to_all(rows, 'z', 0, 0)]
    all_to_all x1 -> x0, waiting for transfers between devices: 10.4 us -> none  [body(): pieces = lax.all_to_all(rows, 'z', 0, 0)]
    all_to_all x1 -> x0, starting transfers between devices: 6.45 us -> none  [body(): pieces = lax.all_to_all(rows, 'z', 0, 0)]
    pallas_call x5 -> x6, Pallas kernels: 12.1 us -> 7.68 us  [the longest x2 6.48 us: project(): pl.pallas_call(project_kernel, grid=(seq // tile,), in_specs=[pl.BlockSpe...]
    add x1, other arithmetic: 1.71 us -> 0.04 us  [body(): rows = (mine + received).reshape(depth, seq // depth, mine.shape[1])]
    broadcast_in_dim x0 -> x1, local copies, waits for them, and re-layouts: none -> 0.73 us  [body(): copies = jnp.broadcast_to(own[None], (groups,) + own.shape)]
  transfers between devices with their start and end apart: 5 -> 4, of which waited for: 4 -> 3; matrix products, arithmetic and copies ran while one was open for 1% -> 0% of each run, Pallas kernels for 7% -> 6%
where the time goes in v2:
time: 60.2 us; the launch traced here: 59.9 us
  blocking collectives  29.2 us (49%)
  starting transfers between devices  15.6 us (26%)
  Pallas kernels  7.68 us (13%)
  waiting for transfers between devices  5.41 us (9%)
  local copies, waits for them, and re-layouts  0.74 us (1%)
  between operations  0.69 us (1%)
    all_to_all x1, blocking collectives, body(): pieces = lax.all_to_all(rows, 'z', 0, 0)  18.6 us
    all_to_all x1, blocking collectives, body(): parts = lax.all_to_all(spread, 'z', 0, 0)  10.6 us
    all_to_all x1, starting transfers between devices, body(): gathered = lax.all_to_all(copies, ('x', 'y'), 0, 0)  6.76 us
    pallas_call x2, Pallas kernels, project(): pl.pallas_call(project_kernel, grid=(seq // tile,), in_specs=[pl.BlockSpe...  6.48 us
    all_to_all x1, waiting for transfers between devices, body(): gathered = lax.all_to_all(copies, ('x', 'y'), 0, 0)  4.34 us
    ppermute x1, starting transfers between devices, body(): received = lax.ppermute(theirs, 'core', SWAP)  3.33 us
    ppermute x1, starting transfers between devices, body(): scores = part + lax.ppermute(part, 'core', SWAP)  3.28 us
    ppermute x1, starting transfers between devices, body(): other = lax.ppermute(own, 'core', SWAP)  2.19 us
  transfers between devices with their start and end apart: 4, of which 3 were waited for; matrix products, arithmetic and copies ran while one was open for 0% of the time, Pallas kernels for 6%

profile of v2, /device:TPU:1, one launch (start us, length us, event | category | flops | bytes accessed | tf_op | source)
XLA Modules:
  0.0 59.9 jit_solution(3692774496533347433)
XLA Ops:
  0.6 3.3 %project.3 = f32[512,128]{1,0:T(8,128)S(1)} custom-call(bf16[2,512,3328]{2,1,0:T(8,128)(2,1)} %grads.3, bf16[2,512,1024]{2,1,0:T(8,128)(2,1)} %acts.3, bf16[64,3328]{1,0:T(8,128)(2,1)} %bitcast.7, bf16[64,1024]{1,0:T(8,128)(2,1)} %bitcast.10), custom_call_target="tpu_custom_call" | custom-call | flops 285212672 | bytes 5275648 | tf_op jit(solution)/shard_map/project/pallas_call | solution.py:39
  3.9 0.0 copy-start
  3.9 0.0 copy-start.1
  3.9 3.3 %collective-permute-start = (f32[512,128]{1,0:T(8,128)S(1)}, f32[512,128]{1,0:T(8,128)S(1)}, u32[]{:S(2)}, u32[]{:S(2)}) collective-permute-start(f32[512,128]{1,0:T(8,128)S(1)} %project.3), channel_id=1, source_target_pairs={{0,1},{1,0},{2,3},{3,2},{4,5},{5,4},{6,7},{7,6},{8,9},{9,8},{10,11... | collective-permute-start | bytes 786440 | tf_op jit(solution)/shard_map/ppermute | solution.py:164
  7.2 3.2 %project.2 = f32[512,128]{1,0:T(8,128)S(1)} custom-call(bf16[2,512,3328]{2,1,0:T(8,128)(2,1)} %grads.3, bf16[2,512,1024]{2,1,0:T(8,128)(2,1)} %acts.3, bf16[64,3328]{1,0:T(8,128)(2,1)} %bitcast.8, bf16[64,1024]{1,0:T(8,128)(2,1)} %bitcast.11), custom_call_target="tpu_custom_call" | custom-call | flops 285212672 | bytes 5275648 | tf_op jit(solution)/shard_map/project/pallas_call | solution.py:39
  10.5 0.0 collective-permute-done
  10.5 18.6 %all_to_all.15.pieces = f32[8,64,128]{2,1,0:T(8,128)S(1)} all-to-all(f32[8,64,128]{2,1,0:T(8,128)S(1)} %bitcast.9), channel_id=1, replica_groups=mesh['x'=4,'y'=4,'z'=8,'core'=2] {'z'}, dimensions={0} | all-to-all | bytes 524288 | tf_op jit(solution)/shard_map/all_to_all | solution.py:167
  29.1 0.0 copy-done
  29.1 0.4 outer.1
  29.6 10.6 %all_to_all.16.pieces = f32[8,32,128]{2,1,0:T(8,128)S(1)} all-to-all(f32[8,32,128]{2,1,0:T(8,128)S(1)} %outer.1), channel_id=1, replica_groups=mesh['x'=4,'y'=4,'z'=8,'core'=2] {'z'}, dimensions={0} | all-to-all | bytes 262144 | tf_op jit(solution)/shard_map/all_to_all | solution.py:169
  40.2 0.7 %broadcast_in_dim.2 = f32[16,32,128]{2,1,0:T(8,128)} broadcast(f32[32,128]{1,0:T(8,128)S(1)} %total.1.own), dimensions={1,2} | broadcast | bytes 278528 | tf_op jit(solution)/shard_map/broadcast_in_dim | solution.py:172
  40.9 6.8 %all-to-all-start.2 = ((f32[16,32,128]{2,1,0:T(8,128)}), f32[16,32,128]{2,1,0:T(8,128)S(1)}, u32[]{:S(2)}, u32[]{:S(2)}) async-start(f32[16,32,128]{2,1,0:T(8,128)} %broadcast_in_dim.2), calls=%async_computation.2 | async-start | bytes 524288 | tf_op jit(solution)/shard_map/all_to_all | solution.py:173
  47.7 2.2 %collective-permute-start.1 = (f32[32,128]{1,0:T(8,128)S(1)}, f32[32,128]{1,0:T(8,128)S(1)}, u32[]{:S(2)}, u32[]{:S(2)}) collective-permute-start(f32[32,128]{1,0:T(8,128)S(1)} %total.1.own), channel_id=1, source_target_pairs={{0,1},{1,0},{2,3},{3,2},{4,5},{5,4},{6,7},{7,6},{8,9},{9,8},{10,11... | collective-permute-start | bytes 49160 | tf_op jit(solution)/shard_map/ppermute | solution.py:171
  49.9 0.8 %collective-permute-done.1.other = f32[32,128]{1,0:T(8,128)S(1)} collective-permute-done((f32[32,128]{1,0:T(8,128)S(1)}, f32[32,128]{1,0:T(8,128)S(1)}, u32[]{:S(2)}, u32[]{:S(2)}) %collective-permute-start.1) | collective-permute-done | bytes 16416 | tf_op jit(solution)/shard_map/ppermute | solution.py:171
  50.7 4.3 %all-to-all-done.2.gathered = f32[16,32,128]{2,1,0:T(8,128)S(1)} async-done(((f32[16,32,128]{2,1,0:T(8,128)}), f32[16,32,128]{2,1,0:T(8,128)S(1)}, u32[]{:S(2)}, u32[]{:S(2)}) %all-to-all-start.2) | async-done | bytes 262176 | tf_op jit(solution)/shard_map/all_to_all | solution.py:173
  55.0 0.0 copy-done.1
  55.0 0.2 score.1
  55.2 3.3 %collective-permute-start.2 = (f32[2,16]{1,0:T(2,128)S(1)}, f32[2,16]{1,0:T(2,128)S(1)}, u32[]{:S(2)}, u32[]{:S(2)}) collective-permute-start(f32[2,16]{1,0:T(2,128)S(1)} %score.1), channel_id=1, source_target_pairs={{0,1},{1,0},{2,3},{3,2},{4,5},{5,4},{6,7},{7,6},{8,9},{9,8},{10,11... | collective-permute-start | bytes 392 | tf_op jit(solution)/shard_map/ppermute | solution.py:176
  58.5 0.6 keep_columns.1
  59.1 0.2 collective-permute-done.2
  59.3 0.6 add.7
  (2 shorter events, 0.1 us)
Async XLA Ops:
  3.9 25.2 %copy-start = (s32[2]{0:T(128)S(1)}, s32[2]{0:T(128)}, u32[]{:S(2)}) copy-start(s32[2]{0:T(128)} %param.10) | copy-start | bytes 28
  3.9 51.1 %copy-start.1 = (s32[16]{0:T(128)S(1)}, s32[16]{0:T(128)}, u32[]{:S(2)}) copy-start(s32[16]{0:T(128)} %param.11) | copy-start | bytes 196
  3.9 6.6 %collective-permute-start = (f32[512,128]{1,0:T(8,128)S(1)}, f32[512,128]{1,0:T(8,128)S(1)}, u32[]{:S(2)}, u32[]{:S(2)}) collective-permute-start(f32[512,128]{1,0:T(8,128)S(1)} %project.3), channel_id=1, source_target_pairs={{0,1},{1,0},{2,3},{3,2},{4,5},{5,4},{6,7},{7,6},{8,9},{9,8},{10,11... | collective-permute-start | bytes 786440 | tf_op jit(solution)/shard_map/ppermute | solution.py:164
  40.9 14.1 %all-to-all-start.2 = ((f32[16,32,128]{2,1,0:T(8,128)}), f32[16,32,128]{2,1,0:T(8,128)S(1)}, u32[]{:S(2)}, u32[]{:S(2)}) async-start(f32[16,32,128]{2,1,0:T(8,128)} %broadcast_in_dim.2), calls=%async_computation.2 | async-start | bytes 524288 | tf_op jit(solution)/shard_map/all_to_all | solution.py:173
  47.7 3.0 %collective-permute-start.1 = (f32[32,128]{1,0:T(8,128)S(1)}, f32[32,128]{1,0:T(8,128)S(1)}, u32[]{:S(2)}, u32[]{:S(2)}) collective-permute-start(f32[32,128]{1,0:T(8,128)S(1)} %total.1.own), channel_id=1, source_target_pairs={{0,1},{1,0},{2,3},{3,2},{4,5},{5,4},{6,7},{7,6},{8,9},{9,8},{10,11... | collective-permute-start | bytes 49160 | tf_op jit(solution)/shard_map/ppermute | solution.py:171
  55.2 4.1 %collective-permute-start.2 = (f32[2,16]{1,0:T(2,128)S(1)}, f32[2,16]{1,0:T(2,128)S(1)}, u32[]{:S(2)}, u32[]{:S(2)}) collective-permute-start(f32[2,16]{1,0:T(2,128)S(1)} %score.1), channel_id=1, source_target_pairs={{0,1},{1,0},{2,3},{3,2},{4,5},{5,4},{6,7},{7,6},{8,9},{9,8},{10,11... | collective-permute-start | bytes 392 | tf_op jit(solution)/shard_map/ppermute | solution.py:176

commit v3 on v2

v3 whole, which is shorter than its diff:
```python
import functools

import jax
import jax.numpy as jnp
from jax import lax
from jax.experimental import pallas as pl
from jax.experimental.pallas import tpu as pltpu
from jax.sharding import Mesh, PartitionSpec as P

F32 = jnp.float32
HIGHEST = lax.Precision.HIGHEST
VMEM_BYTES = 24 * 1024 * 1024
NT = (((1,), (1,)), ((), ()))
TN = (((0,), (0,)), ((), ()))


def vmem():
    return pl.BlockSpec(memory_space=pltpu.VMEM)


def params():
    return pltpu.CompilerParams(vmem_limit_bytes=VMEM_BYTES)


def in_hbm(x):
    return pltpu.with_memory_space_constraint(x, pltpu.HBM)


def project_kernel(grads, acts, w_out, w_in, out):
    rank = w_out.shape[0]
    out[:, rank:] = lax.dot_general(acts[...], w_in[...], NT, preferred_element_type=F32)
    out[:, :rank] = lax.dot_general(grads[...], w_out[...], NT, preferred_element_type=F32)


def project(grads, acts, w_out, w_in, tile):
    rows, width_out = grads.shape
    width_in = acts.shape[1]
    rank = w_out.shape[0]
    return pl.pallas_call(
        project_kernel,
        grid=(rows // tile,),
        in_specs=[
            pl.BlockSpec((tile, width_out), lambda r: (r, 0)),
            pl.BlockSpec((tile, width_in), lambda r: (r, 0)),
            pl.BlockSpec((rank, width_out), lambda r: (0, 0)),
            pl.BlockSpec((rank, width_in), lambda r: (0, 0)),
        ],
        out_specs=pl.BlockSpec((tile, 2 * rank), lambda r: (r, 0)),
        out_shape=jax.ShapeDtypeStruct((rows, 2 * rank), F32),
        compiler_params=params(),
        cost_estimate=pl.CostEstimate(
            flops=2 * rows * rank * (width_in + width_out),
            bytes_accessed=2 * (rows + rank) * (width_in + width_out) + 8 * rows * rank,
            transcendentals=0,
        ),
        name="project",
    )(in_hbm(grads), in_hbm(acts), in_hbm(w_out), in_hbm(w_in))


def outer_kernel(scale, lengths, pieces, out, square):
    rows = jnp.sum(pieces[...], axis=0)
    tokens, width = rows.shape
    rank = width // 2
    core, z = lax.axis_index("core"), lax.axis_index("z")
    count = jnp.where(core == 0, lengths[:, :1], lengths[:, 1:2])
    token = lax.broadcasted_iota(jnp.int32, (tokens, rank), 0) + z * tokens
    keep = (token < count).astype(F32)
    square[...] = scale * lax.dot_general(
        rows[:, :rank] * keep, rows[:, rank:], TN, precision=HIGHEST, preferred_element_type=F32
    )
    even = square[pl.ds(0, rank // 2, stride=2), :]
    odd = square[pl.ds(1, rank // 2, stride=2), :]
    flat = jnp.concatenate([even, odd], axis=1)
    out[...] = jnp.broadcast_to(flat[None], out.shape)


def outer(lengths, pieces, scale):
    shards, _, width = pieces.shape
    rank = width // 2
    return pl.pallas_call(
        functools.partial(outer_kernel, scale),
        in_specs=[vmem(), vmem()],
        out_specs=vmem(),
        out_shape=jax.ShapeDtypeStruct((shards, rank // 2, width), F32),
        scratch_shapes=[pltpu.VMEM((rank, rank), F32)],
        compiler_params=params(),
        name="outer",
    )(lengths.reshape(1, -1), pieces)


def total_kernel(pieces, own):
    own[...] = jnp.sum(pieces[...], axis=0)


def total(pieces):
    return pl.pallas_call(
        total_kernel,
        in_specs=[vmem()],
        out_specs=vmem(),
        out_shape=jax.ShapeDtypeStruct(pieces.shape[1:], F32),
        compiler_params=params(),
        name="total",
    )(pieces)


def finish_kernel(queries, mine, theirs, blocks, scores):
    x, y, z, core = [lax.axis_index(axis) for axis in ("x", "y", "z", "core")]
    groups, rows, _ = mine.shape
    dp = x * lax.axis_size("y") + y
    group = lax.broadcasted_iota(jnp.int32, (groups, queries.shape[1]), 0)
    asked = queries[...]
    select = (2 * group + core == asked).astype(F32)
    select_other = (2 * group + 1 - core == asked).astype(F32)
    first, second = mine[...], theirs[...]
    for e in range(2):
        pick = core == e
        own = jnp.where(pick, mine[dp], theirs[dp])
        dots = jnp.sum(jnp.sum(first * own[None], axis=1), axis=1, keepdims=True)
        other = jnp.sum(jnp.sum(second * own[None], axis=1), axis=1, keepdims=True)
        total = jnp.sum(dots * select + other * select_other, axis=0, keepdims=True)
        scores[pl.ds(e, 1), :] = total / (2 * rows)
        place = 2 * (2 * z + core)
        cut = [
            jnp.where(pick, mine[dp, pl.ds(place + k, 1), :], theirs[dp, pl.ds(place + k, 1), :])
            for k in range(2)
        ]
        blocks[pl.ds(e, 1), :] = jnp.concatenate(cut, axis=1)


def finish(queries, mine, theirs):
    return pl.pallas_call(
        finish_kernel,
        in_specs=[vmem()] * 3,
        out_specs=[vmem()] * 2,
        out_shape=[
            jax.ShapeDtypeStruct((2, 2 * mine.shape[2]), F32),
            jax.ShapeDtypeStruct((2, queries.shape[0]), F32),
        ],
        compiler_params=params(),
        name="finish",
    )(queries.reshape(1, -1), mine, theirs)


SWAP = [(0, 1), (1, 0)]


def body(acts, grads, proj_in, proj_out, lengths, queries):
    seq = acts.shape[1]
    depth = lax.axis_size("z")
    groups = lax.axis_size("x") * lax.axis_size("y")
    core = lax.axis_index("core")
    part = project(
        grads.reshape(-1, grads.shape[2]), acts.reshape(-1, acts.shape[2]), proj_out.T, proj_in.T, seq
    ).reshape(acts.shape[0], seq, -1)
    received = lax.ppermute(lax.dynamic_index_in_dim(part, 1 - core, 0, False), "core", SWAP)
    rows = lax.dynamic_index_in_dim(part, core, 0, False) + received
    rows = rows.reshape(depth, seq // depth, rows.shape[1])
    pieces = lax.all_to_all(rows, "z", 0, 0)
    spread = outer(lengths, pieces, seq ** (-0.5))
    parts = lax.all_to_all(spread, "z", 0, 0)
    own = total(parts)
    copies = jnp.broadcast_to(own[None], (groups,) + own.shape)
    gathered = lax.all_to_all(copies, ("x", "y"), 0, 0)
    received = lax.ppermute(gathered, "core", SWAP)
    return tuple(finish(queries, gathered, received))


def solution(mesh):
    devices = mesh.devices.reshape(4, 4, 8, 2)
    dp, tensor = ("x", "y"), ("z", "core")
    return jax.shard_map(
        body,
        mesh=Mesh(devices, dp + tensor),
        in_specs=(
            P(dp, None, tensor),
            P(dp, None, tensor),
            P(tensor, None),
            P(tensor, None),
            P(dp),
            P(),
        ),
        out_specs=(P(dp, tensor), P(dp, None)),
        check_vma=False,
    )
```

time: 60.2 us -> 58.7 us (0.975)
  blocking collectives: 29.2 us -> 41.5 us
  starting transfers between devices: 15.6 us -> 7.65 us
  waiting for transfers between devices: 5.41 us -> 2.32 us
  Pallas kernels: 7.68 us -> 6.28 us
  local copies, waits for them, and re-layouts: 0.74 us -> 0.06 us
    all_to_all x0 -> x1, blocking collectives: none -> 13.9 us  [body(): gathered = lax.all_to_all(copies, ('x', 'y'), 0, 0)]
    all_to_all x1 -> x0, starting transfers between devices: 6.76 us -> none  [body(): gathered = lax.all_to_all(copies, ('x', 'y'), 0, 0)]
    all_to_all x1 -> x0, waiting for transfers between devices: 4.34 us -> none  [body(): gathered = lax.all_to_all(copies, ('x', 'y'), 0, 0)]
    pallas_call x4 -> x2, Pallas kernels: 7.23 us -> 5.83 us  [the longest x1 5.04 us: project(): pl.pallas_call(project_kernel, grid=(rows // tile,), in_specs=[pl.BlockSp...]
    all_to_all x1, blocking collectives: 18.6 us -> 17.3 us  [body(): pieces = lax.all_to_all(rows, 'z', 0, 0)]
    ppermute x3 -> x2, waiting for transfers between devices: 1.07 us -> 2.32 us  [the longest x1 1.16 us: body(): received = lax.ppermute(gathered, 'core', SWAP)]
    ppermute x3 -> x2, starting transfers between devices: 8.8 us -> 7.65 us  [the longest x1 4.33 us: body(): received = lax.ppermute(gathered, 'core', SWAP)]
    broadcast_in_dim x1, local copies, waits for them, and re-layouts: 0.73 us -> 0.02 us  [body(): copies = jnp.broadcast_to(own[None], (groups,) + own.shape)]
  transfers between devices with their start and end apart: 4 -> 2, of which waited for: 3 -> 2; matrix products, arithmetic and copies ran while one was open for 0% -> 0% of each run, Pallas kernels for 6% -> 0%
where the time goes in v3:
time: 58.7 us; the launch traced here: 58.5 us
  blocking collectives  41.5 us (71%)
  starting transfers between devices  7.65 us (13%)
  Pallas kernels  6.28 us (11%)
  waiting for transfers between devices  2.32 us (4%)
  between operations  0.68 us (1%)
    all_to_all x1, blocking collectives, body(): pieces = lax.all_to_all(rows, 'z', 0, 0)  17.3 us
    all_to_all x1, blocking collectives, body(): gathered = lax.all_to_all(copies, ('x', 'y'), 0, 0)  13.9 us
    all_to_all x1, blocking collectives, body(): parts = lax.all_to_all(spread, 'z', 0, 0)  10.3 us
    pallas_call x1, Pallas kernels, project(): pl.pallas_call(project_kernel, grid=(rows // tile,), in_specs=[pl.BlockSp...  5.04 us
    ppermute x1, starting transfers between devices, body(): received = lax.ppermute(gathered, 'core', SWAP)  4.33 us
    ppermute x1, starting transfers between devices, body(): lax.ppermute(lax.dynamic_index_in_dim(part, 1 - core, 0, False), 'core',...  3.33 us
  transfers between devices with their start and end apart: 2, of which 2 were waited for; matrix products, arithmetic and copies ran while one was open for 0% of the time, Pallas kernels for 0%

profile of v3, /device:TPU:1, one launch (start us, length us, event | category | flops | bytes accessed | tf_op | source)
XLA Modules:
  0.0 58.5 jit_solution(8984029459056864438)
XLA Ops:
  0.6 0.0 copy-start
  0.6 0.0 copy-start.1
  0.7 5.0 %project.1 = f32[1024,128]{1,0:T(8,128)S(1)} custom-call(bf16[1024,3328]{1,0:T(8,128)(2,1)} %bitcast.16, bf16[1024,1024]{1,0:T(8,128)(2,1)} %bitcast.17, bf16[64,3328]{1,0:T(8,128)(2,1)} %bitcast.19, bf16[64,1024]{1,0:T(8,128)(2,1)} %bitcast.20), custom_call_target="tpu_custom_call" | custom-call | flops 570425344 | bytes 9994240 | tf_op jit(solution)/shard_map/project/pallas_call | solution.py:39
  5.7 3.3 %collective-permute-start = (f32[512,128]{1,0:T(8,128)S(1)}, f32[512,128]{1,0:T(8,128)S(1)}, u32[]{:S(2)}, u32[]{:S(2)}) collective-permute-start(f32[512,128]{1,0:T(8,128)S(1)} %dynamic-slice_bitcast_fusion), channel_id=1, source_target_pairs={{0,1},{1,0},{2,3},{3,2},{4,5},{5,4},{6,7},{7,6},{8,9},{9,8},{10,11... | collective-permute-start | bytes 786440 | tf_op jit(solution)/shard_map/ppermute | solution.py:155
  9.1 1.2 %collective-permute-done = f32[512,128]{1,0:T(8,128)S(1)} collective-permute-done((f32[512,128]{1,0:T(8,128)S(1)}, f32[512,128]{1,0:T(8,128)S(1)}, u32[]{:S(2)}, u32[]{:S(2)}) %collective-permute-start) | collective-permute-done | bytes 262176 | tf_op jit(solution)/shard_map/ppermute | solution.py:155
  10.3 17.3 %all_to_all.15.pieces = f32[8,64,128]{2,1,0:T(8,128)S(1)} all-to-all(f32[8,64,128]{2,1,0:T(8,128)S(1)} %bitcast.18), channel_id=1, replica_groups=mesh['x'=4,'y'=4,'z'=8,'core'=2] {'z'}, dimensions={0} | all-to-all | bytes 524288 | tf_op jit(solution)/shard_map/all_to_all | solution.py:158
  27.6 0.0 copy-done
  27.6 0.4 outer.1
  28.0 10.3 %all_to_all.16.pieces = f32[8,32,128]{2,1,0:T(8,128)S(1)} all-to-all(f32[8,32,128]{2,1,0:T(8,128)S(1)} %outer.1), channel_id=1, replica_groups=mesh['x'=4,'y'=4,'z'=8,'core'=2] {'z'}, dimensions={0} | all-to-all | bytes 262144 | tf_op jit(solution)/shard_map/all_to_all | solution.py:160
  38.4 13.9 %all_to_all.17.mine = f32[16,32,128]{2,1,0:T(8,128)S(1)} all-to-all(f32[16,32,128]{2,1,0:T(8,128)S(1)} %broadcast_in_dim.2), channel_id=1, replica_groups=mesh['x'=4,'y'=4,'z'=8,'core'=2] {'x','y'}, dimensions={0} | all-to-all | bytes 524288 | tf_op jit(solution)/shard_map/all_to_all | solution.py:163
  52.3 4.3 %collective-permute-start.1 = (f32[16,32,128]{2,1,0:T(8,128)S(1)}, f32[16,32,128]{2,1,0:T(8,128)S(1)}, u32[]{:S(2)}, u32[]{:S(2)}) collective-permute-start(f32[16,32,128]{2,1,0:T(8,128)S(1)} %all_to_all.17.mine), channel_id=1, source_target_pairs={{0,1},{1,0},{2,3},{3,2},{4,5},{5,4},{6,7},{7,6},{8,9},{9,8},{10,11... | collective-permute-start | bytes 786440 | tf_op jit(solution)/shard_map/ppermute | solution.py:164
  56.6 1.2 %collective-permute-done.1.theirs = f32[16,32,128]{2,1,0:T(8,128)S(1)} collective-permute-done((f32[16,32,128]{2,1,0:T(8,128)S(1)}, f32[16,32,128]{2,1,0:T(8,128)S(1)}, u32[]{:S(2)}, u32[]{:S(2)}) %collective-permute-start.1) | collective-permute-done | bytes 262176 | tf_op jit(solution)/shard_map/ppermute | solution.py:164
  57.8 0.0 copy-done.1
  57.8 0.8 %finish.1 = (f32[2,256]{1,0:T(2,128)}, f32[2,16]{1,0:T(2,128)}) custom-call(s32[1,16]{1,0:T(1,128)S(1)} %bitcast.15, f32[16,32,128]{2,1,0:T(8,128)S(1)} %all_to_all.17.mine, f32[16,32,128]{2,1,0:T(8,128)S(1)} %collective-permute-done.1.theirs), custom_call_target="tpu_custom_call" | custom-call | tf_op jit(solution)/shard_map/finish/pallas_call | solution.py:131
  (4 shorter events, 0.1 us)
Async XLA Ops:
  0.6 27.0 %copy-start = (s32[2]{0:T(128)S(1)}, s32[2]{0:T(128)}, u32[]{:S(2)}) copy-start(s32[2]{0:T(128)} %param.10) | copy-start | bytes 28
  0.6 57.1 %copy-start.1 = (s32[16]{0:T(128)S(1)}, s32[16]{0:T(128)}, u32[]{:S(2)}) copy-start(s32[16]{0:T(128)} %param.11) | copy-start | bytes 196
  5.7 4.5 %collective-permute-start = (f32[512,128]{1,0:T(8,128)S(1)}, f32[512,128]{1,0:T(8,128)S(1)}, u32[]{:S(2)}, u32[]{:S(2)}) collective-permute-start(f32[512,128]{1,0:T(8,128)S(1)} %dynamic-slice_bitcast_fusion), channel_id=1, source_target_pairs={{0,1},{1,0},{2,3},{3,2},{4,5},{5,4},{6,7},{7,6},{8,9},{9,8},{10,11... | collective-permute-start | bytes 786440 | tf_op jit(solution)/shard_map/ppermute | solution.py:155
  52.3 5.5 %collective-permute-start.1 = (f32[16,32,128]{2,1,0:T(8,128)S(1)}, f32[16,32,128]{2,1,0:T(8,128)S(1)}, u32[]{:S(2)}, u32[]{:S(2)}) collective-permute-start(f32[16,32,128]{2,1,0:T(8,128)S(1)} %all_to_all.17.mine), channel_id=1, source_target_pairs={{0,1},{1,0},{2,3},{3,2},{4,5},{5,4},{6,7},{7,6},{8,9},{9,8},{10,11... | collective-permute-start | bytes 786440 | tf_op jit(solution)/shard_map/ppermute | solution.py:164

commit v4 on v3

--- a/solution.py
+++ b/solution.py
@@ -12,6 +12,16 @@
 VMEM_BYTES = 24 * 1024 * 1024
 NT = (((1,), (1,)), ((), ()))
 TN = (((0,), (0,)), ((), ()))
+Z_ORDER = (4, 0, 5, 1, 6, 2, 7, 3)
+XY_ORDER = (10, 11, 12, 13, 14, 15, 0, 1, 2, 3, 4, 5, 6, 7, 8, 9)
+
+
+def place_in(order, index):
+    return sum(jnp.where(index == held, place, 0) for place, held in enumerate(order))
+
+
+def exchange(x, axes, order):
+    return lax.all_to_all(x, axes, 0, 0, axis_index_groups=[list(order)])
 
 
 def vmem():
@@ -61,9 +71,10 @@
     rows = jnp.sum(pieces[...], axis=0)
     tokens, width = rows.shape
     rank = width // 2
-    core, z = lax.axis_index("core"), lax.axis_index("z")
+    core = lax.axis_index("core")
+    chunk = place_in(Z_ORDER, lax.axis_index("z"))
     count = jnp.where(core == 0, lengths[:, :1], lengths[:, 1:2])
-    token = lax.broadcasted_iota(jnp.int32, (tokens, rank), 0) + z * tokens
+    token = lax.broadcasted_iota(jnp.int32, (tokens, rank), 0) + chunk * tokens
     keep = (token < count).astype(F32)
     square[...] = scale * lax.dot_general(
         rows[:, :rank] * keep, rows[:, rank:], TN, precision=HIGHEST, preferred_element_type=F32
@@ -106,8 +117,10 @@
 def finish_kernel(queries, mine, theirs, blocks, scores):
     x, y, z, core = [lax.axis_index(axis) for axis in ("x", "y", "z", "core")]
     groups, rows, _ = mine.shape
-    dp = x * lax.axis_size("y") + y
-    group = lax.broadcasted_iota(jnp.int32, (groups, queries.shape[1]), 0)
+    dp = place_in(XY_ORDER, x * lax.axis_size("y") + y)
+    shape = (groups, queries.shape[1])
+    held = lax.broadcasted_iota(jnp.int32, shape, 0) + XY_ORDER[0]
+    group = jnp.where(held >= groups, held - groups, held)
     asked = queries[...]
     select = (2 * group + core == asked).astype(F32)
     select_other = (2 * group + 1 - core == asked).astype(F32)
@@ -155,12 +168,12 @@
     received = lax.ppermute(lax.dynamic_index_in_dim(part, 1 - core, 0, False), "core", SWAP)
     rows = lax.dynamic_index_in_dim(part, core, 0, False) + received
     rows = rows.reshape(depth, seq // depth, rows.shape[1])
-    pieces = lax.all_to_all(rows, "z", 0, 0)
+    pieces = exchange(rows, "z", Z_ORDER)
     spread = outer(lengths, pieces, seq ** (-0.5))
-    parts = lax.all_to_all(spread, "z", 0, 0)
+    parts = exchange(spread, "z", Z_ORDER)
     own = total(parts)
     copies = jnp.broadcast_to(own[None], (groups,) + own.shape)
-    gathered = lax.all_to_all(copies, ("x", "y"), 0, 0)
+    gathered = exchange(copies, ("x", "y"), XY_ORDER)
     received = lax.ppermute(gathered, "core", SWAP)
     return tuple(finish(queries, gathered, received))
 

time: 58.7 us -> 51.3 us (0.87)
  blocking collectives: 41.5 us -> 35.1 us
  starting transfers between devices: 7.65 us -> 6.61 us
    all_to_all x3, blocking collectives: 41.5 us -> 35.1 us  [exchange(): return lax.all_to_all(x, axes, 0, 0, axis_index_groups=[list(order)])]
    ppermute x1, starting transfers between devices: 4.33 us -> 3.28 us  [body(): received = lax.ppermute(gathered, 'core', SWAP)]
where the time goes in v4:
time: 51.3 us; the launch traced here: 51.1 us
  blocking collectives  35.1 us (68%)
  starting transfers between devices  6.61 us (13%)
  Pallas kernels  6.27 us (12%)
  waiting for transfers between devices  2.32 us (5%)
  between operations  0.68 us (1%)
    all_to_all x3, blocking collectives, exchange(): return lax.all_to_all(x, axes, 0, 0, axis_index_groups=[list(order)])  35.1 us
    pallas_call x1, Pallas kernels, project(): pl.pallas_call(project_kernel, grid=(rows // tile,), in_specs=[pl.BlockSp...  5.04 us
    ppermute x1, starting transfers between devices, body(): lax.ppermute(lax.dynamic_index_in_dim(part, 1 - core, 0, False), 'core',...  3.33 us
    ppermute x1, starting transfers between devices, body(): received = lax.ppermute(gathered, 'core', SWAP)  3.28 us
    ppermute x1, waiting for transfers between devices, body(): received = lax.ppermute(gathered, 'core', SWAP)  1.16 us
    ppermute x1, waiting for transfers between devices, body(): lax.ppermute(lax.dynamic_index_in_dim(part, 1 - core, 0, False), 'core',...  1.16 us
  transfers between devices with their start and end apart: 2, of which 2 were waited for; matrix products, arithmetic and copies ran while one was open for 0% of the time, Pallas kernels for 0%

profile of v4, /device:TPU:1, one launch (start us, length us, event | category | flops | bytes accessed | tf_op | source)
XLA Modules:
  0.0 51.1 jit_solution(3839255540581720097)
XLA Ops:
  0.6 0.0 copy-start
  0.6 0.0 copy-start.1
  0.7 5.0 %project.1 = f32[1024,128]{1,0:T(8,128)S(1)} custom-call(bf16[1024,3328]{1,0:T(8,128)(2,1)} %bitcast.16, bf16[1024,1024]{1,0:T(8,128)(2,1)} %bitcast.17, bf16[64,3328]{1,0:T(8,128)(2,1)} %bitcast.19, bf16[64,1024]{1,0:T(8,128)(2,1)} %bitcast.20), custom_call_target="tpu_custom_call" | custom-call | flops 570425344 | bytes 9994240 | tf_op jit(solution)/shard_map/project/pallas_call | solution.py:49
  5.7 3.3 %collective-permute-start = (f32[512,128]{1,0:T(8,128)S(1)}, f32[512,128]{1,0:T(8,128)S(1)}, u32[]{:S(2)}, u32[]{:S(2)}) collective-permute-start(f32[512,128]{1,0:T(8,128)S(1)} %dynamic-slice_bitcast_fusion), channel_id=1, source_target_pairs={{0,1},{1,0},{2,3},{3,2},{4,5},{5,4},{6,7},{7,6},{8,9},{9,8},{10,11... | collective-permute-start | bytes 786440 | tf_op jit(solution)/shard_map/ppermute | solution.py:168
  9.1 1.2 %collective-permute-done = f32[512,128]{1,0:T(8,128)S(1)} collective-permute-done((f32[512,128]{1,0:T(8,128)S(1)}, f32[512,128]{1,0:T(8,128)S(1)}, u32[]{:S(2)}, u32[]{:S(2)}) %collective-permute-start) | collective-permute-done | bytes 262176 | tf_op jit(solution)/shard_map/ppermute | solution.py:168
  10.3 13.8 %all_to_all.15.pieces = f32[8,64,128]{2,1,0:T(8,128)S(1)} all-to-all(f32[8,64,128]{2,1,0:T(8,128)S(1)} %bitcast.18), channel_id=1, replica_groups={{8,0,10,2,12,4,14,6},{9,1,11,3,13,5,15,7},{24,16,26,18,28,20,30,22},{25..., dimensions={0} | all-to-all | bytes 524288 | tf_op jit(solution)/shard_map/all_to_all | solution.py:24
  24.0 0.0 copy-done
  24.0 0.4 outer.1
  24.5 10.5 %all_to_all.16.pieces = f32[8,32,128]{2,1,0:T(8,128)S(1)} all-to-all(f32[8,32,128]{2,1,0:T(8,128)S(1)} %outer.1), channel_id=1, replica_groups={{8,0,10,2,12,4,14,6},{9,1,11,3,13,5,15,7},{24,16,26,18,28,20,30,22},{25..., dimensions={0} | all-to-all | bytes 262144 | tf_op jit(solution)/shard_map/all_to_all | solution.py:24
  35.0 10.9 %all_to_all.17.mine = f32[16,32,128]{2,1,0:T(8,128)S(1)} all-to-all(f32[16,32,128]{2,1,0:T(8,128)S(1)} %broadcast_in_dim.2), channel_id=1, replica_groups={{160,176,192,208,224,240,0,16,32,48,64,80,96,112,128,144},{161,177,193,..., dimensions={0} | all-to-all | bytes 524288 | tf_op jit(solution)/shard_map/all_to_all | solution.py:24
  45.9 3.3 %collective-permute-start.1 = (f32[16,32,128]{2,1,0:T(8,128)S(1)}, f32[16,32,128]{2,1,0:T(8,128)S(1)}, u32[]{:S(2)}, u32[]{:S(2)}) collective-permute-start(f32[16,32,128]{2,1,0:T(8,128)S(1)} %all_to_all.17.mine), channel_id=1, source_target_pairs={{0,1},{1,0},{2,3},{3,2},{4,5},{5,4},{6,7},{7,6},{8,9},{9,8},{10,11... | collective-permute-start | bytes 786440 | tf_op jit(solution)/shard_map/ppermute | solution.py:177
  49.2 1.2 %collective-permute-done.1.theirs = f32[16,32,128]{2,1,0:T(8,128)S(1)} collective-permute-done((f32[16,32,128]{2,1,0:T(8,128)S(1)}, f32[16,32,128]{2,1,0:T(8,128)S(1)}, u32[]{:S(2)}, u32[]{:S(2)}) %collective-permute-start.1) | collective-permute-done | bytes 262176 | tf_op jit(solution)/shard_map/ppermute | solution.py:177
  50.3 0.0 copy-done.1
  50.3 0.8 %finish.1 = (f32[2,256]{1,0:T(2,128)}, f32[2,16]{1,0:T(2,128)}) custom-call(s32[1,16]{1,0:T(1,128)S(1)} %bitcast.15, f32[16,32,128]{2,1,0:T(8,128)S(1)} %all_to_all.17.mine, f32[16,32,128]{2,1,0:T(8,128)S(1)} %collective-permute-done.1.theirs), custom_call_target="tpu_custom_call" | custom-call | tf_op jit(solution)/shard_map/finish/pallas_call | solution.py:144
  (4 shorter events, 0.1 us)
Async XLA Ops:
  0.6 23.4 %copy-start = (s32[2]{0:T(128)S(1)}, s32[2]{0:T(128)}, u32[]{:S(2)}) copy-start(s32[2]{0:T(128)} %param.10) | copy-start | bytes 28
  0.6 49.7 %copy-start.1 = (s32[16]{0:T(128)S(1)}, s32[16]{0:T(128)}, u32[]{:S(2)}) copy-start(s32[16]{0:T(128)} %param.11) | copy-start | bytes 196
  5.7 4.5 %collective-permute-start = (f32[512,128]{1,0:T(8,128)S(1)}, f32[512,128]{1,0:T(8,128)S(1)}, u32[]{:S(2)}, u32[]{:S(2)}) collective-permute-start(f32[512,128]{1,0:T(8,128)S(1)} %dynamic-slice_bitcast_fusion), channel_id=1, source_target_pairs={{0,1},{1,0},{2,3},{3,2},{4,5},{5,4},{6,7},{7,6},{8,9},{9,8},{10,11... | collective-permute-start | bytes 786440 | tf_op jit(solution)/shard_map/ppermute | solution.py:168
  45.9 4.4 %collective-permute-start.1 = (f32[16,32,128]{2,1,0:T(8,128)S(1)}, f32[16,32,128]{2,1,0:T(8,128)S(1)}, u32[]{:S(2)}, u32[]{:S(2)}) collective-permute-start(f32[16,32,128]{2,1,0:T(8,128)S(1)} %all_to_all.17.mine), channel_id=1, source_target_pairs={{0,1},{1,0},{2,3},{3,2},{4,5},{5,4},{6,7},{7,6},{8,9},{9,8},{10,11... | collective-permute-start | bytes 786440 | tf_op jit(solution)/shard_map/ppermute | solution.py:177

commit v5 on v4

--- a/solution.py
+++ b/solution.py
@@ -12,7 +12,7 @@
 VMEM_BYTES = 24 * 1024 * 1024
 NT = (((1,), (1,)), ((), ()))
 TN = (((0,), (0,)), ((), ()))
-Z_ORDER = (4, 0, 5, 1, 6, 2, 7, 3)
+Z_ORDER = (4, 0, 1, 7, 2, 6, 3, 5)
 XY_ORDER = (10, 11, 12, 13, 14, 15, 0, 1, 2, 3, 4, 5, 6, 7, 8, 9)
 
 

time: 51.3 us -> 51.2 us (level)
  no operation moved by 1% of the time
where the time goes in v5:
time: 51.2 us; the launch traced here: 51 us
  blocking collectives  34.7 us (68%)
  starting transfers between devices  6.93 us (14%)
  Pallas kernels  6.27 us (12%)
  waiting for transfers between devices  2.32 us (5%)
  between operations  0.68 us (1%)
    all_to_all x3, blocking collectives, exchange(): return lax.all_to_all(x, axes, 0, 0, axis_index_groups=[list(order)])  34.7 us
    pallas_call x1, Pallas kernels, project(): pl.pallas_call(project_kernel, grid=(rows // tile,), in_specs=[pl.BlockSp...  5.04 us
    ppermute x1, starting transfers between devices, body(): received = lax.ppermute(gathered, 'core', SWAP)  3.6 us
    ppermute x1, starting transfers between devices, body(): lax.ppermute(lax.dynamic_index_in_dim(part, 1 - core, 0, False), 'core',...  3.33 us
    ppermute x1, waiting for transfers between devices, body(): received = lax.ppermute(gathered, 'core', SWAP)  1.16 us
    ppermute x1, waiting for transfers between devices, body(): lax.ppermute(lax.dynamic_index_in_dim(part, 1 - core, 0, False), 'core',...  1.16 us
  transfers between devices with their start and end apart: 2, of which 2 were waited for; matrix products, arithmetic and copies ran while one was open for 0% of the time, Pallas kernels for 0%

profile of v5, /device:TPU:1, one launch (start us, length us, event | category | flops | bytes accessed | tf_op | source)
XLA Modules:
  0.0 51.0 jit_solution(1503804482714820608)
XLA Ops:
  0.6 0.0 copy-start
  0.6 0.0 copy-start.1
  0.7 5.0 %project.1 = f32[1024,128]{1,0:T(8,128)S(1)} custom-call(bf16[1024,3328]{1,0:T(8,128)(2,1)} %bitcast.16, bf16[1024,1024]{1,0:T(8,128)(2,1)} %bitcast.17, bf16[64,3328]{1,0:T(8,128)(2,1)} %bitcast.19, bf16[64,1024]{1,0:T(8,128)(2,1)} %bitcast.20), custom_call_target="tpu_custom_call" | custom-call | flops 570425344 | bytes 9994240 | tf_op jit(solution)/shard_map/project/pallas_call | solution.py:49
  5.7 3.3 %collective-permute-start = (f32[512,128]{1,0:T(8,128)S(1)}, f32[512,128]{1,0:T(8,128)S(1)}, u32[]{:S(2)}, u32[]{:S(2)}) collective-permute-start(f32[512,128]{1,0:T(8,128)S(1)} %dynamic-slice_bitcast_fusion), channel_id=1, source_target_pairs={{0,1},{1,0},{2,3},{3,2},{4,5},{5,4},{6,7},{7,6},{8,9},{9,8},{10,11... | collective-permute-start | bytes 786440 | tf_op jit(solution)/shard_map/ppermute | solution.py:168
  9.1 1.2 %collective-permute-done = f32[512,128]{1,0:T(8,128)S(1)} collective-permute-done((f32[512,128]{1,0:T(8,128)S(1)}, f32[512,128]{1,0:T(8,128)S(1)}, u32[]{:S(2)}, u32[]{:S(2)}) %collective-permute-start) | collective-permute-done | bytes 262176 | tf_op jit(solution)/shard_map/ppermute | solution.py:168
  10.3 13.6 %all_to_all.15.pieces = f32[8,64,128]{2,1,0:T(8,128)S(1)} all-to-all(f32[8,64,128]{2,1,0:T(8,128)S(1)} %bitcast.18), channel_id=1, replica_groups={{8,0,2,14,4,12,6,10},{9,1,3,15,5,13,7,11},{24,16,18,30,20,28,22,26},{25..., dimensions={0} | all-to-all | bytes 524288 | tf_op jit(solution)/shard_map/all_to_all | solution.py:24
  23.8 0.0 copy-done
  23.8 0.4 outer.1
  24.3 10.3 %all_to_all.16.pieces = f32[8,32,128]{2,1,0:T(8,128)S(1)} all-to-all(f32[8,32,128]{2,1,0:T(8,128)S(1)} %outer.1), channel_id=1, replica_groups={{8,0,2,14,4,12,6,10},{9,1,3,15,5,13,7,11},{24,16,18,30,20,28,22,26},{25..., dimensions={0} | all-to-all | bytes 262144 | tf_op jit(solution)/shard_map/all_to_all | solution.py:24
  34.6 10.9 %all_to_all.17.mine = f32[16,32,128]{2,1,0:T(8,128)S(1)} all-to-all(f32[16,32,128]{2,1,0:T(8,128)S(1)} %broadcast_in_dim.2), channel_id=1, replica_groups={{160,176,192,208,224,240,0,16,32,48,64,80,96,112,128,144},{161,177,193,..., dimensions={0} | all-to-all | bytes 524288 | tf_op jit(solution)/shard_map/all_to_all | solution.py:24
  45.5 3.6 %collective-permute-start.1 = (f32[16,32,128]{2,1,0:T(8,128)S(1)}, f32[16,32,128]{2,1,0:T(8,128)S(1)}, u32[]{:S(2)}, u32[]{:S(2)}) collective-permute-start(f32[16,32,128]{2,1,0:T(8,128)S(1)} %all_to_all.17.mine), channel_id=1, source_target_pairs={{0,1},{1,0},{2,3},{3,2},{4,5},{5,4},{6,7},{7,6},{8,9},{9,8},{10,11... | collective-permute-start | bytes 786440 | tf_op jit(solution)/shard_map/ppermute | solution.py:177
  49.1 1.2 %collective-permute-done.1.theirs = f32[16,32,128]{2,1,0:T(8,128)S(1)} collective-permute-done((f32[16,32,128]{2,1,0:T(8,128)S(1)}, f32[16,32,128]{2,1,0:T(8,128)S(1)}, u32[]{:S(2)}, u32[]{:S(2)}) %collective-permute-start.1) | collective-permute-done | bytes 262176 | tf_op jit(solution)/shard_map/ppermute | solution.py:177
  50.2 0.0 copy-done.1
  50.2 0.8 %finish.1 = (f32[2,256]{1,0:T(2,128)}, f32[2,16]{1,0:T(2,128)}) custom-call(s32[1,16]{1,0:T(1,128)S(1)} %bitcast.15, f32[16,32,128]{2,1,0:T(8,128)S(1)} %all_to_all.17.mine, f32[16,32,128]{2,1,0:T(8,128)S(1)} %collective-permute-done.1.theirs), custom_call_target="tpu_custom_call" | custom-call | tf_op jit(solution)/shard_map/finish/pallas_call | solution.py:144
  (4 shorter events, 0.1 us)
Async XLA Ops:
  0.6 23.2 %copy-start = (s32[2]{0:T(128)S(1)}, s32[2]{0:T(128)}, u32[]{:S(2)}) copy-start(s32[2]{0:T(128)} %param.10) | copy-start | bytes 28
  0.6 49.6 %copy-start.1 = (s32[16]{0:T(128)S(1)}, s32[16]{0:T(128)}, u32[]{:S(2)}) copy-start(s32[16]{0:T(128)} %param.11) | copy-start | bytes 196
  5.7 4.5 %collective-permute-start = (f32[512,128]{1,0:T(8,128)S(1)}, f32[512,128]{1,0:T(8,128)S(1)}, u32[]{:S(2)}, u32[]{:S(2)}) collective-permute-start(f32[512,128]{1,0:T(8,128)S(1)} %dynamic-slice_bitcast_fusion), channel_id=1, source_target_pairs={{0,1},{1,0},{2,3},{3,2},{4,5},{5,4},{6,7},{7,6},{8,9},{9,8},{10,11... | collective-permute-start | bytes 786440 | tf_op jit(solution)/shard_map/ppermute | solution.py:168
  45.5 4.8 %collective-permute-start.1 = (f32[16,32,128]{2,1,0:T(8,128)S(1)}, f32[16,32,128]{2,1,0:T(8,128)S(1)}, u32[]{:S(2)}, u32[]{:S(2)}) collective-permute-start(f32[16,32,128]{2,1,0:T(8,128)S(1)} %all_to_all.17.mine), channel_id=1, source_target_pairs={{0,1},{1,0},{2,3},{3,2},{4,5},{5,4},{6,7},{7,6},{8,9},{9,8},{10,11... | collective-permute-start | bytes 786440 | tf_op jit(solution)/shard_map/ppermute | solution.py:177

commit v6 on v5

--- a/solution.py
+++ b/solution.py
@@ -114,25 +114,50 @@
     )(pieces)
 
 
-def finish_kernel(queries, mine, theirs, blocks, scores):
-    x, y, z, core = [lax.axis_index(axis) for axis in ("x", "y", "z", "core")]
+def chosen(queries, core, groups):
+    held = lax.broadcasted_iota(jnp.int32, (groups, queries.shape[1]), 0) + XY_ORDER[0]
+    group = jnp.where(held >= groups, held - groups, held)
+    return (2 * group + core == queries[...]).astype(F32)
+
+
+def dot_with(blocks, own, select):
+    dots = jnp.sum(jnp.sum(blocks * own[None], axis=1), axis=1, keepdims=True)
+    return jnp.sum(dots * select, axis=0, keepdims=True)
+
+
+def own_place():
+    return place_in(XY_ORDER, lax.axis_index("x") * lax.axis_size("y") + lax.axis_index("y"))
+
+
+def begin_kernel(queries, mine, out):
+    select = chosen(queries, lax.axis_index("core"), mine.shape[0])
+    out[...] = dot_with(mine[...], mine[own_place()], select)
+
+
+def begin(queries, mine):
+    return pl.pallas_call(
+        begin_kernel,
+        in_specs=[vmem()] * 2,
+        out_specs=vmem(),
+        out_shape=jax.ShapeDtypeStruct((1, queries.shape[0]), F32),
+        compiler_params=params(),
+        name="begin",
+    )(queries.reshape(1, -1), mine)
+
+
+def finish_kernel(queries, begun, mine, theirs, blocks, scores):
+    z, core = lax.axis_index("z"), lax.axis_index("core")
     groups, rows, _ = mine.shape
-    dp = place_in(XY_ORDER, x * lax.axis_size("y") + y)
-    shape = (groups, queries.shape[1])
-    held = lax.broadcasted_iota(jnp.int32, shape, 0) + XY_ORDER[0]
-    group = jnp.where(held >= groups, held - groups, held)
-    asked = queries[...]
-    select = (2 * group + core == asked).astype(F32)
-    select_other = (2 * group + 1 - core == asked).astype(F32)
+    dp = own_place()
+    select = chosen(queries, core, groups)
+    select_other = chosen(queries, 1 - core, groups)
     first, second = mine[...], theirs[...]
+    my_row = begun[...] + dot_with(second, mine[dp], select_other)
+    their_row = dot_with(first, theirs[dp], select) + dot_with(second, theirs[dp], select_other)
+    place = 2 * (2 * z + core)
     for e in range(2):
         pick = core == e
-        own = jnp.where(pick, mine[dp], theirs[dp])
-        dots = jnp.sum(jnp.sum(first * own[None], axis=1), axis=1, keepdims=True)
-        other = jnp.sum(jnp.sum(second * own[None], axis=1), axis=1, keepdims=True)
-        total = jnp.sum(dots * select + other * select_other, axis=0, keepdims=True)
-        scores[pl.ds(e, 1), :] = total / (2 * rows)
-        place = 2 * (2 * z + core)
+        scores[pl.ds(e, 1), :] = jnp.where(pick, my_row, their_row) / (2 * rows)
         cut = [
             jnp.where(pick, mine[dp, pl.ds(place + k, 1), :], theirs[dp, pl.ds(place + k, 1), :])
             for k in range(2)
@@ -140,10 +165,10 @@
         blocks[pl.ds(e, 1), :] = jnp.concatenate(cut, axis=1)
 
 
-def finish(queries, mine, theirs):
+def finish(queries, begun, mine, theirs):
     return pl.pallas_call(
         finish_kernel,
-        in_specs=[vmem()] * 3,
+        in_specs=[vmem()] * 4,
         out_specs=[vmem()] * 2,
         out_shape=[
             jax.ShapeDtypeStruct((2, 2 * mine.shape[2]), F32),
@@ -151,7 +176,7 @@
         ],
         compiler_params=params(),
         name="finish",
-    )(queries.reshape(1, -1), mine, theirs)
+    )(queries.reshape(1, -1), begun, mine, theirs)
 
 
 SWAP = [(0, 1), (1, 0)]
@@ -175,7 +200,7 @@
     copies = jnp.broadcast_to(own[None], (groups,) + own.shape)
     gathered = exchange(copies, ("x", "y"), XY_ORDER)
     received = lax.ppermute(gathered, "core", SWAP)
-    return tuple(finish(queries, gathered, received))
+    return tuple(finish(queries, begin(queries, gathered), gathered, received))
 
 
 def solution(mesh):

time: 51.2 us -> 51.2 us (level)
  no operation moved by 1% of the time
where the time goes in v6:
time: 51.2 us; the launch traced here: 51 us
  blocking collectives  34.7 us (68%)
  starting transfers between devices  6.93 us (14%)
  Pallas kernels  6.38 us (12%)
  waiting for transfers between devices  2.18 us (4%)
  between operations  0.68 us (1%)
    all_to_all x3, blocking collectives, exchange(): return lax.all_to_all(x, axes, 0, 0, axis_index_groups=[list(order)])  34.7 us
    pallas_call x1, Pallas kernels, project(): pl.pallas_call(project_kernel, grid=(rows // tile,), in_specs=[pl.BlockSp...  5.04 us
    ppermute x1, starting transfers between devices, body(): received = lax.ppermute(gathered, 'core', SWAP)  3.6 us
    ppermute x1, starting transfers between devices, body(): lax.ppermute(lax.dynamic_index_in_dim(part, 1 - core, 0, False), 'core',...  3.33 us
    ppermute x1, waiting for transfers between devices, body(): lax.ppermute(lax.dynamic_index_in_dim(part, 1 - core, 0, False), 'core',...  1.16 us
  transfers between devices with their start and end apart: 2, of which 2 were waited for; matrix products, arithmetic and copies ran while one was open for 0% of the time, Pallas kernels for 0%

profile of v6, /device:TPU:1, one launch (start us, length us, event | category | flops | bytes accessed | tf_op | source)
XLA Modules:
  0.0 51.0 jit_solution(903992684443346690)
XLA Ops:
  0.6 0.0 copy-start.1
  0.6 0.0 copy-start
  0.7 5.0 %project.1 = f32[1024,128]{1,0:T(8,128)S(1)} custom-call(bf16[1024,3328]{1,0:T(8,128)(2,1)} %bitcast.17, bf16[1024,1024]{1,0:T(8,128)(2,1)} %bitcast.18, bf16[64,3328]{1,0:T(8,128)(2,1)} %bitcast.20, bf16[64,1024]{1,0:T(8,128)(2,1)} %bitcast.21), custom_call_target="tpu_custom_call" | custom-call | flops 570425344 | bytes 9994240 | tf_op jit(solution)/shard_map/project/pallas_call | solution.py:49
  5.7 3.3 %collective-permute-start = (f32[512,128]{1,0:T(8,128)S(1)}, f32[512,128]{1,0:T(8,128)S(1)}, u32[]{:S(2)}, u32[]{:S(2)}) collective-permute-start(f32[512,128]{1,0:T(8,128)S(1)} %dynamic-slice_bitcast_fusion), channel_id=1, source_target_pairs={{0,1},{1,0},{2,3},{3,2},{4,5},{5,4},{6,7},{7,6},{8,9},{9,8},{10,11... | collective-permute-start | bytes 786440 | tf_op jit(solution)/shard_map/ppermute | solution.py:193
  9.1 1.2 %collective-permute-done = f32[512,128]{1,0:T(8,128)S(1)} collective-permute-done((f32[512,128]{1,0:T(8,128)S(1)}, f32[512,128]{1,0:T(8,128)S(1)}, u32[]{:S(2)}, u32[]{:S(2)}) %collective-permute-start) | collective-permute-done | bytes 262176 | tf_op jit(solution)/shard_map/ppermute | solution.py:193
  10.3 13.6 %all_to_all.15.pieces = f32[8,64,128]{2,1,0:T(8,128)S(1)} all-to-all(f32[8,64,128]{2,1,0:T(8,128)S(1)} %bitcast.19), channel_id=1, replica_groups={{8,0,2,14,4,12,6,10},{9,1,3,15,5,13,7,11},{24,16,18,30,20,28,22,26},{25..., dimensions={0} | all-to-all | bytes 524288 | tf_op jit(solution)/shard_map/all_to_all | solution.py:24
  23.8 0.0 copy-done.1
  23.8 0.4 outer.1
  24.3 10.3 %all_to_all.16.pieces = f32[8,32,128]{2,1,0:T(8,128)S(1)} all-to-all(f32[8,32,128]{2,1,0:T(8,128)S(1)} %outer.1), channel_id=1, replica_groups={{8,0,2,14,4,12,6,10},{9,1,3,15,5,13,7,11},{24,16,18,30,20,28,22,26},{25..., dimensions={0} | all-to-all | bytes 262144 | tf_op jit(solution)/shard_map/all_to_all | solution.py:24
  34.6 10.9 %all_to_all.17.mine = f32[16,32,128]{2,1,0:T(8,128)S(1)} all-to-all(f32[16,32,128]{2,1,0:T(8,128)S(1)} %broadcast_in_dim.2), channel_id=1, replica_groups={{160,176,192,208,224,240,0,16,32,48,64,80,96,112,128,144},{161,177,193,..., dimensions={0} | all-to-all | bytes 524288 | tf_op jit(solution)/shard_map/all_to_all | solution.py:24
  45.5 3.6 %collective-permute-start.1 = (f32[16,32,128]{2,1,0:T(8,128)S(1)}, f32[16,32,128]{2,1,0:T(8,128)S(1)}, u32[]{:S(2)}, u32[]{:S(2)}) collective-permute-start(f32[16,32,128]{2,1,0:T(8,128)S(1)} %all_to_all.17.mine), channel_id=1, source_target_pairs={{0,1},{1,0},{2,3},{3,2},{4,5},{5,4},{6,7},{7,6},{8,9},{9,8},{10,11... | collective-permute-start | bytes 786440 | tf_op jit(solution)/shard_map/ppermute | solution.py:202
  49.1 0.0 copy-done
  49.1 0.1 begin.1.begun
  49.2 1.0 %collective-permute-done.1.theirs = f32[16,32,128]{2,1,0:T(8,128)S(1)} collective-permute-done((f32[16,32,128]{2,1,0:T(8,128)S(1)}, f32[16,32,128]{2,1,0:T(8,128)S(1)}, u32[]{:S(2)}, u32[]{:S(2)}) %collective-permute-start.1) | collective-permute-done | bytes 262176 | tf_op jit(solution)/shard_map/ppermute | solution.py:202
  50.2 0.7 %finish.1 = (f32[2,256]{1,0:T(2,128)}, f32[2,16]{1,0:T(2,128)}) custom-call(s32[1,16]{1,0:T(1,128)S(1)} %bitcast.15, f32[1,16]{1,0:T(1,128)S(1)} %begin.1.begun, f32[16,32,128]{2,1,0:T(8,128)S(1)} %all_to_all.17.mine, f32[16,32,128]{2,1,0:T(8,128)S(1)} %collective-permute-done.1.theirs), custom_call_target="tpu_custom_call" | custom-call | tf_op jit(solution)/shard_map/finish/pallas_call | solution.py:169
  (4 shorter events, 0.1 us)
Async XLA Ops:
  0.6 23.2 %copy-start.1 = (s32[2]{0:T(128)S(1)}, s32[2]{0:T(128)}, u32[]{:S(2)}) copy-start(s32[2]{0:T(128)} %param.10) | copy-start | bytes 28
  0.6 48.4 %copy-start = (s32[16]{0:T(128)S(1)}, s32[16]{0:T(128)}, u32[]{:S(2)}) copy-start(s32[16]{0:T(128)} %param.11) | copy-start | bytes 196
  5.7 4.5 %collective-permute-start = (f32[512,128]{1,0:T(8,128)S(1)}, f32[512,128]{1,0:T(8,128)S(1)}, u32[]{:S(2)}, u32[]{:S(2)}) collective-permute-start(f32[512,128]{1,0:T(8,128)S(1)} %dynamic-slice_bitcast_fusion), channel_id=1, source_target_pairs={{0,1},{1,0},{2,3},{3,2},{4,5},{5,4},{6,7},{7,6},{8,9},{9,8},{10,11... | collective-permute-start | bytes 786440 | tf_op jit(solution)/shard_map/ppermute | solution.py:193
  45.5 4.8 %collective-permute-start.1 = (f32[16,32,128]{2,1,0:T(8,128)S(1)}, f32[16,32,128]{2,1,0:T(8,128)S(1)}, u32[]{:S(2)}, u32[]{:S(2)}) collective-permute-start(f32[16,32,128]{2,1,0:T(8,128)S(1)} %all_to_all.17.mine), channel_id=1, source_target_pairs={{0,1},{1,0},{2,3},{3,2},{4,5},{5,4},{6,7},{7,6},{8,9},{9,8},{10,11... | collective-permute-start | bytes 786440 | tf_op jit(solution)/shard_map/ppermute | solution.py:202
